TPU v7x, 32 devices: a whole 2x2x4 slice. The times are simulated.
32 devices in a mesh: ma: 8 (over z, x), band: 4 (over y, core).
Axes of the slice: x: 2, y: 2, z: 4, core: 2. Of those that a mesh axis runs over, the one named last changes fastest.
Arguments:
- harmonics: bfloat16 [32, 8192, 256], P(('ma', 'band')), may hold values from -6 to 6
- legendre: bfloat16 [32, 2, 8192, 128], P(('ma', 'band')), may hold values from -0.005859375 to 0.005859375
- m_values: int32 [32], replicated, may hold values from 1 to 8191
- cycle_cell: int32 [4096], P(('ma', 'band')), may hold values from 0 to 31, as said below
- phi_cell: int32 [4096], P(('ma', 'band')), may hold values from 3 to 123
- offsets: float32 [2, 4096], P(None, ('ma', 'band')), may hold values from 0 to 1
Outputs:
- lensed: float32 [4096, 128], P(('ma', 'band'))
Inputs may be any that keep to these rules, and one draw needn't show every extreme that they name: `cycle_cell`: Band-local cycle; every point held by device (ma, band) lies in latitude band `band`. For each device and each ma index q, at most 16 of its points have cycles q * 4 to q * 4 + 3, and in every band one q receives exactly 16 points from every device of the band.
All inputs are finite; a program needn't handle non-finite values.
Results may differ from a plain program's by a relative error of at most 0.0053.
Values may be sent and summed in bfloat16 or wider, within the bound.
A program may use at most 64 MiB of HBM per device.

v0:
```python
import functools
import math

import jax
import jax.numpy as jnp
from jax import lax
from jax.experimental import pallas as pl
from jax.experimental.pallas import tpu as pltpu
from jax.sharding import PartitionSpec as P

NPHI = 128
LANES = 128
TAPS = 8
MESH = pl.DeviceIdType.MESH
F32 = jnp.float32
BF16 = jnp.bfloat16


def quotient(value, by):
    return value >> (by.bit_length() - 1) if by & (by - 1) == 0 else lax.div(value, by)


def remainder(value, by):
    return value & (by - 1) if by & (by - 1) == 0 else lax.rem(value, by)


def short_sine(y):
    square = y * y
    series = 0.0
    for n in (13, 11, 9, 7, 5, 3):
        series = (series + (-1.0) ** (n // 2) / math.factorial(n)) * square
    return y + y * series


def turn_sine(turn, period):
    turn = jnp.where(turn > period // 2, turn - period, turn)
    turn = jnp.where(turn > period // 4, period // 2 - turn, turn)
    turn = jnp.where(turn < -(period // 4), -(period // 2) - turn, turn)
    return short_sine(turn.astype(F32) * (2.0 * math.pi / period))


def taps_of(offset_row):
    tap = lax.broadcasted_iota(jnp.int32, (TAPS, offset_row.shape[1]), 0)
    shifts = tap.astype(F32) - 3.0 - offset_row
    whole = short_sine(math.pi * jnp.minimum(offset_row, 1.0 - offset_row))
    whole = jnp.where(remainder(tap, 2) == 1, -whole, whole)
    quarter = shifts / 4.0
    mirrored = jnp.where(quarter > 0.5, 1.0 - quarter, quarter)
    mirrored = jnp.where(quarter < -0.5, -1.0 - quarter, mirrored)
    wide = short_sine(math.pi * mirrored)
    zero = shifts == 0.0
    safe = jnp.where(zero, 1.0, shifts) * math.pi
    return jnp.where(zero, 1.0, (whole / safe) * (wide / (safe / 4.0)))


def kernel(
    dims, harm, leg, m_in, cell_in, phi_in, off_in, out_ref,
    harm_v, leg_v, acc, pts, phase, picks, acrosses, besides, mixed, weights, send, recv, back, ret,
    m_ref, cell_ref, phi_ref, off_ref, load_sems, small_sems, pts_send, pts_recv, spec_send, spec_recv, ret_send, ret_recv,
):
    owners, bands, depth, period, chunk, prebuilt = dims
    total = owners * bands
    length, columns = harm.shape
    cycles = leg.shape[2]
    evolutions = columns // 4
    width = 2 * evolutions
    rows = cycles // bands
    share = width // owners
    pieces = length // chunk
    pack = LANES // (2 * rows)
    lines = share // pack
    ma = lax.axis_index("ma")
    band = lax.axis_index("band")
    me = ma * bands + band
    group = total // 4
    slab = group * 2 * rows
    my_group = quotient(me, group)
    order = [
        my_group,
        my_group + 1 - 2 * remainder(my_group, 2),
        my_group + 2 - 4 * quotient(my_group, 2),
        3 - my_group,
    ]

    def loads(step):
        here = pl.ds(step * chunk if isinstance(step, int) else pl.multiple_of(step * chunk, chunk), chunk)
        pairs = [(harm.at[here], harm_v.at[here])]
        for half in range(2):
            pairs.append((leg.at[half, here], leg_v.at[here, pl.ds(half * cycles, cycles)]))
        return [
            pltpu.make_async_copy(src, dst, load_sems.at[n, step])
            for n, (src, dst) in enumerate(pairs)
        ]

    def start_loads(step, carry):
        for copy in loads(step):
            copy.start()
        return carry

    lax.fori_loop(0, 1, start_loads, 0)
    small = [
        pltpu.make_async_copy(src, dst, small_sems.at[n])
        for n, (src, dst) in enumerate(
            [(off_in, off_ref), (cell_in, cell_ref), (phi_in, phi_ref), (m_in, m_ref)]
        )
    ]
    for copy in small:
        copy.start()
    lax.fori_loop(1, pieces, start_loads, 0)

    barrier = pltpu.get_barrier_semaphore()

    def greet(step, carry):
        peer = remainder(me + step, total)
        pl.semaphore_signal(
            barrier, inc=1, device_id=(quotient(peer, bands), remainder(peer, bands)),
            device_id_type=MESH,
        )
        return carry

    lax.fori_loop(1, total, greet, 0)

    for copy in small:
        copy.wait()

    pts[ma, 0:TAPS, :] = taps_of(off_ref[0:1, :])
    pts[ma, TAPS:2 * TAPS, :] = taps_of(off_ref[1:2, :])
    row = lax.broadcasted_iota(jnp.int32, (TAPS, LANES), 0)
    pts[ma, 2 * TAPS:3 * TAPS, :] = jnp.where(
        row == 0, cell_ref[...], jnp.where(row == 1, phi_ref[...], 0)
    ).astype(F32)

    eye = lax.broadcasted_iota(jnp.int32, (total, total), 0) == lax.broadcasted_iota(
        jnp.int32, (total, total), 1
    )
    m_column = jnp.sum(jnp.where(eye, m_ref[...].astype(F32), 0.0), axis=1, keepdims=True)
    pixel = lax.broadcasted_iota(jnp.int32, (total, NPHI), 1)
    turns = remainder(m_column.astype(jnp.int32) * pixel, period)
    quarter_on = remainder(turns + period // 4, period)
    phase[0:total, :] = turn_sine(quarter_on, period).astype(BF16)
    phase[total:2 * total, :] = (-turn_sine(turns, period)).astype(BF16)

    lane = lax.broadcasted_iota(jnp.int32, (1, LANES), 1)
    inner = remainder(lane, 2 * rows)
    j = remainder(inner, rows)
    place = quotient(inner, rows) * cycles + quotient(j, depth) * (bands * depth) + remainder(j, depth)
    away = lax.broadcasted_iota(jnp.int32, (2 * cycles, LANES), 0) - place
    for b in range(bands):
        picks[:, b * LANES:(b + 1) * LANES] = jnp.where(away == b * depth, 1.0, 0.0).astype(BF16)

    acc[...] = jnp.zeros_like(acc)

    def multiply(step, carry):
        for copy in loads(step):
            copy.wait()
        here = pl.ds(step * chunk, chunk)
        acc[...] += lax.dot_general(
            harm_v[here, :], leg_v[here, :], (((0,), (0,)), ((), ())),
            preferred_element_type=F32,
        )
        return carry

    for step in range(pieces // 4):
        multiply(step, 0)

    pl.semaphore_wait(barrier, total - 1)

    def send_points(step, carry):
        peer = remainder(ma + step, owners)
        pltpu.make_async_remote_copy(
            src_ref=pts.at[ma], dst_ref=pts.at[ma], send_sem=pts_send, recv_sem=pts_recv,
            device_id=(peer, band), device_id_type=MESH,
        ).start()
        return carry

    lax.fori_loop(1, owners, send_points, 0)

    for step in range(pieces // 4, pieces):
        multiply(step, 0)

    def part(half, which):
        return acc[which * evolutions:(which + 1) * evolutions, half * cycles:(half + 1) * cycles]

    q_real = -(part(0, 0) - part(1, 3))
    q_imag = -(part(0, 1) + part(1, 2))
    u_real = -(part(0, 2) + part(1, 1))
    u_imag = -(part(0, 3) - part(1, 0))
    real = jnp.concatenate([q_real, u_real], axis=0)
    imag = jnp.concatenate([q_imag, u_imag], axis=0)
    spectra = jnp.concatenate([real, imag], axis=1).astype(BF16)

    moved = jnp.dot(spectra, picks[...], preferred_element_type=F32)
    first = quotient(lane, 2 * rows) == remainder(me, pack)
    for b in range(bands):
        band_part = moved[:, b * LANES:(b + 1) * LANES]
        for q in range(owners):
            block = band_part[q * share:q * share + lines]
            if pack == 2:
                block = jnp.where(first, block, band_part[q * share + lines:(q + 1) * share])
            send[b, q] = block.astype(BF16)

    for n in (3, 2, 1, 0):
        def send_spectra(step, carry):
            peer = order[n] * group + remainder(me + step, group)
            to_ma, to_band = quotient(peer, bands), remainder(peer, bands)
            pltpu.make_async_remote_copy(
                src_ref=send.at[to_band, to_ma], dst_ref=recv.at[me], send_sem=spec_send,
                recv_sem=spec_recv.at[my_group], device_id=(to_ma, to_band),
                device_id_type=MESH,
            ).start()
            return carry

        lax.fori_loop(1 if n == 0 else 0, group, send_spectra, 0)
    recv[me] = send[band, ma]

    others = pl.ds(0, owners - 1)
    pltpu.make_async_copy(pts.at[others], pts.at[others], pts_recv).wait()

    def spread(s, column):
        pixels = lax.broadcasted_iota(jnp.int32, (NPHI, LANES), 0)
        ring = lax.broadcasted_iota(jnp.int32, (rows, LANES), 0)
        table = pts[s]
        cell = table[2 * TAPS:2 * TAPS + 1].astype(jnp.int32)
        phi = table[2 * TAPS + 1:2 * TAPS + 2].astype(jnp.int32)
        across = jnp.zeros((rows, LANES), F32)
        beside = jnp.zeros((NPHI, LANES), F32)
        for e in range(TAPS):
            across = jnp.where(ring == cell + (e - 3), table[e:e + 1], across)
            beside = jnp.where(pixels == phi + (e - 3), table[TAPS + e:TAPS + e + 1], beside)
        high = beside.astype(BF16)
        acrosses[:, column] = across
        besides[0:NPHI, column] = high
        besides[NPHI:2 * NPHI, column] = (beside - high.astype(F32)).astype(BF16)

    def mix():
        mixed[...] = jnp.dot(
            jnp.concatenate([phase[...], phase[...]], axis=1), besides[...],
            preferred_element_type=F32,
        )

    def build(column):
        across = acrosses[:, column]
        factors = mixed[:, column]
        for g in range(total):
            for i in range(2):
                at = (g * 2 + i) * rows
                weights[at:at + rows, column] = (
                    factors[i * total + g:i * total + g + 1] * across
                ).astype(BF16)

    def block_of(s):
        return pl.ds(pl.multiple_of(s * LANES, LANES), LANES)

    def spread_one(s, carry):
        spread(s, block_of(s))
        return carry

    def build_one(s, carry):
        build(block_of(s))
        return carry

    if prebuilt:
        lax.fori_loop(0, owners, spread_one, 0, unroll=4)
        mix()
        lax.fori_loop(0, owners, build_one, 0, unroll=2)

    def arrive(n):
        came = pl.ds(0, group - 1 if n == 0 else group)
        pltpu.make_async_copy(recv.at[came], recv.at[came], spec_recv.at[order[n]]).wait()

    low_half = lax.broadcasted_iota(jnp.int32, (lines, LANES), 1) < LANES // 2

    def lined(at):
        blocks = []
        for h in range(group // pack):
            block = recv[at * group + h * pack].astype(F32)
            if pack == 2:
                other = recv[at * group + h * pack + 1].astype(F32)
                upper = jnp.where(low_half, other, block)
                block = jnp.concatenate(
                    [jnp.where(low_half, block, other), pltpu.roll(upper, LANES // 2, 1)], axis=0
                )
            blocks.append(block.astype(BF16))
        return jnp.concatenate(blocks, axis=1)

    def give(t, values):
        for half in range(2):
            s = 2 * t + half
            back[s] = values[:, half * LANES:(half + 1) * LANES].astype(back.dtype)

            @pl.when(s != ma)
            def _():
                pltpu.make_async_remote_copy(
                    src_ref=back.at[s], dst_ref=ret.at[ma], send_sem=ret_send,
                    recv_sem=ret_recv, device_id=(s, band), device_id_type=MESH,
                ).start()

    if prebuilt:
        pairs = order[::-1] if owners == 8 else list(range(owners // 2))
        sums = [0.0] * len(pairs)
        for n in range(4):
            arrive(n)
            left = lined(order[n])
            here = pl.ds(pl.multiple_of(order[n] * slab, slab), slab)
            for k, t in enumerate(pairs):
                both = pl.ds(pl.multiple_of(t * (2 * LANES), 2 * LANES), 2 * LANES)
                sums[k] += jnp.dot(left, weights[here, both], preferred_element_type=F32)
                if n == 3:
                    give(t, sums[k])
    else:
        for n in range(4):
            arrive(n)
        left = jnp.concatenate([lined(n) for n in range(4)], axis=1)
        for t in range(owners // 2):
            for half in range(2):
                spread(2 * t + half, pl.ds(half * LANES, LANES))
            mix()
            for half in range(2):
                build(pl.ds(half * LANES, LANES))
            give(t, jnp.dot(left, weights[...], preferred_element_type=F32))

    ret[ma] = back[ma]
    pltpu.make_async_copy(ret.at[others], ret.at[others], ret_recv).wait()
    out_ref[...] = ret[...].astype(F32).reshape(width, LANES).T

    pltpu.make_async_copy(pts.at[others], pts.at[others], pts_send).wait()
    arrived = pl.ds(0, total - 1)
    pltpu.make_async_copy(recv.at[arrived], recv.at[arrived], spec_send).wait()
    pltpu.make_async_copy(back.at[others], back.at[others], ret_send).wait()


def on_device(harmonics, legendre, m_values, cycle_cell, phi_cell, offsets):
    owners, bands = lax.axis_size("ma"), lax.axis_size("band")
    total = owners * bands
    _, length, columns = harmonics.shape
    cycles = legendre.shape[3]
    width = columns // 2
    rows = cycles // bands
    share = width // owners
    points = cycle_cell.shape[0]
    depth = cycles // total
    pack = LANES // (2 * rows)
    chunk = min(1024, length)
    pieces = length // chunk
    contraction = total * 2 * rows
    prebuilt = contraction * owners * points * 2 <= 16 * 2**20
    kept = owners * points if prebuilt else 2 * points
    wire = BF16 if share % 16 == 0 else F32
    dims = (owners, bands, depth, 2 * length, chunk, prebuilt)
    vmem = pl.BlockSpec(memory_space=pltpu.VMEM)
    far = pl.BlockSpec(memory_space=pltpu.HBM)
    dma = pltpu.SemaphoreType.DMA
    halved = pl.pallas_call(
        functools.partial(kernel, dims),
        out_shape=jax.ShapeDtypeStruct((points, width), F32),
        in_specs=[far] * 6,
        out_specs=vmem,
        scratch_shapes=[
            pltpu.VMEM((length, columns), BF16),
            pltpu.VMEM((length, 2 * cycles), BF16),
            pltpu.VMEM((columns, 2 * cycles), F32),
            pltpu.VMEM((owners, 3 * TAPS, points), F32),
            pltpu.VMEM((2 * total, NPHI), BF16),
            pltpu.VMEM((2 * cycles, bands * LANES), BF16),
            pltpu.VMEM((rows, kept), F32),
            pltpu.VMEM((2 * NPHI, kept), BF16),
            pltpu.VMEM((2 * total, kept), F32),
            pltpu.VMEM((contraction, kept), BF16),
            pltpu.VMEM((bands, owners, share // pack, LANES), BF16),
            pltpu.VMEM((total, share // pack, LANES), BF16),
            pltpu.VMEM((owners, share, points), wire),
            pltpu.VMEM((owners, share, points), wire),
            pltpu.VMEM((1, total), jnp.int32),
            pltpu.VMEM((1, points), jnp.int32),
            pltpu.VMEM((1, points), jnp.int32),
            pltpu.VMEM((2, points), F32),
            dma((3, pieces)),
            dma((4,)),
            dma, dma, dma, dma((4,)), dma, dma,
        ],
        compiler_params=pltpu.CompilerParams(
            collective_id=0, has_side_effects=True, vmem_limit_bytes=(20 if prebuilt else 56) * 2**20
        ),
    )(
        *[
            pltpu.with_memory_space_constraint(x, pltpu.HBM)
            for x in (
                harmonics[0], legendre[0], m_values.reshape(1, -1), cycle_cell.reshape(1, -1),
                phi_cell.reshape(1, -1), offsets,
            )
        ]
    )
    return 2.0 * halved


def solution(mesh):
    in_specs = (
        P(("ma", "band"), None, None),
        P(("ma", "band"), None, None, None),
        P(),
        P(("ma", "band")),
        P(("ma", "band")),
        P(None, ("ma", "band")),
    )
    out_specs = P(("ma", "band"), None)
    return jax.shard_map(
        on_device, mesh=mesh, in_specs=in_specs, out_specs=out_specs, check_vma=False
    )
```

profile of v0, /device:TPU:0, one launch (start us, length us, event | category | flops | bytes accessed | tf_op | source)
XLA Modules:
  0.0 20.6 jit_solution(6741939504038904491)
XLA Ops:
  0.0 20.0 %shard_map.64 = f32[128,128]{1,0:T(8,128)S(1)} custom-call(bf16[8192,256]{1,0:T(8,128)(2,1)} %bitcast.5, bf16[2,8192,128]{2,1,0:T(8,128)(2,1)} %bitcast.6, s32[1,32]{1,0:T(1,128)} %bitcast.7, s32[1,128]{1,0:T(1,128)} %bitcast.8, s32[1,128]{1,0:T(1,128)} %bitcast.9, f32[2,128]{1,0:T(2,128)} %off_in.1), custom_call_target="tpu_custom_call" | custom-call | tf_op jit(solution)/shard_map/pallas_call | solution.py:353
  20.0 0.6 %broadcast_multiply_fusion = f32[128,128]{1,0:T(8,128)} fusion(f32[128,128]{1,0:T(8,128)S(1)} %shard_map.64), kind=kLoop, calls=%fused_computation | loop fusion | flops 16384 | bytes 131072 | tf_op jit(solution)/shard_map/mul | solution.py:393
where the time goes:
time: 20.8 us; the launch traced here: 20.6 us
  Pallas kernels  20 us (96%)
  other arithmetic  0.64 us (3%)
    pallas_call x1, Pallas kernels, on_device(): pl.pallas_call(functools.partial(kernel, dims), out_shape=jax.ShapeDtypeS...  20 us
    mul x1, other arithmetic, on_device(): return 2.0 * halved  0.64 us

commit v1 on v0

--- a/solution.py
+++ b/solution.py
@@ -22,6 +22,14 @@
 
 def remainder(value, by):
     return value & (by - 1) if by & (by - 1) == 0 else lax.rem(value, by)
+
+
+def repeat(begin, end, body):
+    if end - begin <= 32:
+        for step in range(begin, end):
+            body(step, 0)
+    else:
+        lax.fori_loop(begin, end, body, 0)
 
 
 def short_sine(y):
@@ -97,7 +105,7 @@
             copy.start()
         return carry
 
-    lax.fori_loop(0, 1, start_loads, 0)
+    repeat(0, 1, start_loads)
     small = [
         pltpu.make_async_copy(src, dst, small_sems.at[n])
         for n, (src, dst) in enumerate(
@@ -106,7 +114,7 @@
     ]
     for copy in small:
         copy.start()
-    lax.fori_loop(1, pieces, start_loads, 0)
+    repeat(1, pieces, start_loads)
 
     barrier = pltpu.get_barrier_semaphore()
 
@@ -118,7 +126,7 @@
         )
         return carry
 
-    lax.fori_loop(1, total, greet, 0)
+    repeat(1, total, greet)
 
     for copy in small:
         copy.wait()
@@ -160,7 +168,7 @@
         )
         return carry
 
-    for step in range(pieces // 4):
+    for step in range(pieces // 2):
         multiply(step, 0)
 
     pl.semaphore_wait(barrier, total - 1)
@@ -173,9 +181,9 @@
         ).start()
         return carry
 
-    lax.fori_loop(1, owners, send_points, 0)
-
-    for step in range(pieces // 4, pieces):
+    repeat(1, owners, send_points)
+
+    for step in range(pieces // 2, pieces):
         multiply(step, 0)
 
     def part(half, which):
@@ -210,7 +218,7 @@
             ).start()
             return carry
 
-        lax.fori_loop(1 if n == 0 else 0, group, send_spectra, 0)
+        repeat(1 if n == 0 else 0, group, send_spectra)
     recv[me] = send[band, ma]
 
     others = pl.ds(0, owners - 1)

time: 20.8 us -> 21.1 us (1.014)
  Pallas kernels: 20 us -> 20.3 us
    pallas_call x1, Pallas kernels: 20 us -> 20.3 us  [on_device(): pl.pallas_call(functools.partial(kernel, dims), out_shape=jax.ShapeDtypeS...]
where the time goes in v1:
time: 21.1 us; the launch traced here: 20.9 us
  Pallas kernels  20.3 us (96%)
  other arithmetic  0.64 us (3%)
    pallas_call x1, Pallas kernels, on_device(): pl.pallas_call(functools.partial(kernel, dims), out_shape=jax.ShapeDtypeS...  20.3 us
    mul x1, other arithmetic, on_device(): return 2.0 * halved  0.64 us

profile of v1, /device:TPU:0, one launch (start us, length us, event | category | flops | bytes accessed | tf_op | source)
XLA Modules:
  0.0 20.9 jit_solution(9911774076759317237)
XLA Ops:
  0.0 20.3 %shard_map.64 = f32[128,128]{1,0:T(8,128)S(1)} custom-call(bf16[8192,256]{1,0:T(8,128)(2,1)} %bitcast.5, bf16[2,8192,128]{2,1,0:T(8,128)(2,1)} %bitcast.6, s32[1,32]{1,0:T(1,128)} %bitcast.7, s32[1,128]{1,0:T(1,128)} %bitcast.8, s32[1,128]{1,0:T(1,128)} %bitcast.9, f32[2,128]{1,0:T(2,128)} %off_in.1), custom_call_target="tpu_custom_call" | custom-call | tf_op jit(solution)/shard_map/pallas_call | solution.py:361
  20.3 0.6 %broadcast_multiply_fusion = f32[128,128]{1,0:T(8,128)} fusion(f32[128,128]{1,0:T(8,128)S(1)} %shard_map.64), kind=kLoop, calls=%fused_computation | loop fusion | flops 16384 | bytes 131072 | tf_op jit(solution)/shard_map/mul | solution.py:401
